TPU v7x, 32 devices: a whole 2x2x4 slice. The times are simulated.
32 devices in a mesh: seq: 8 (over z, x), dp: 4 (over y, core).
Axes of the slice: x: 2, y: 2, z: 4, core: 2. Of those that a mesh axis runs over, the one named last changes fastest.
Arguments:
- tokens: bfloat16 [4, 1024, 2048], P('dp', 'seq'), may hold values from -6 to 6
- out_grad: bfloat16 [4, 1024, 2048], P('dp', 'seq'), may hold values from -6 to 6
- span_order: int32 [16], replicated, may hold values from 0 to 15, each once
- doc_starts: int32 [4, 8], P('dp'), may hold values from 0 to 1023, as said below
- w_query: bfloat16 [2048, 2048], P(('seq', 'dp')), may hold values from -0.125 to 0.125
- w_key: bfloat16 [2048, 1024], P(('seq', 'dp')), may hold values from -0.125 to 0.125
- w_value: bfloat16 [2048, 1024], P(('seq', 'dp')), may hold values from -0.125 to 0.125
- w_output: bfloat16 [2048, 2048], P(('seq', 'dp')), may hold values from -2 to 2
- attn_gain: float32 [2048], P(('seq', 'dp')), may hold values from 0.5 to 1.5
- query_gain: float32 [128], replicated, may hold values from 0.5 to 1.5
- key_gain: float32 [128], replicated, may hold values from 0.5 to 1.5
- w_gate: bfloat16 [2048, 6144], P(('seq', 'dp')), may hold values from -0.125 to 0.125
- w_up: bfloat16 [2048, 6144], P(('seq', 'dp')), may hold values from -0.125 to 0.125
- w_down: bfloat16 [2048, 6144], P(('seq', 'dp')), may hold values from -0.078125 to 0.078125
- mlp_gain: float32 [2048], P(('seq', 'dp')), may hold values from 0.5 to 1.5
Outputs:
- block_out: bfloat16 [4, 1024, 2048], P('dp', 'seq')
- tokens_grad: float32 [4, 1024, 2048], P('dp', 'seq')
- w_query_grad: float32 [2048, 2048], P(('seq', 'dp'))
- w_key_grad: float32 [2048, 1024], P(('seq', 'dp'))
- w_value_grad: float32 [2048, 1024], P(('seq', 'dp'))
- w_output_grad: float32 [2048, 2048], P(('seq', 'dp'))
- attn_gain_grad: float32 [2048], P(('seq', 'dp'))
- query_gain_grad: float32 [128], replicated
- key_gain_grad: float32 [128], replicated
- w_gate_grad: float32 [2048, 6144], P(('seq', 'dp'))
- w_up_grad: float32 [2048, 6144], P(('seq', 'dp'))
- w_down_grad: float32 [2048, 6144], P(('seq', 'dp'))
- mlp_gain_grad: float32 [2048], P(('seq', 'dp'))
Inputs may be any that keep to these rules, and one draw needn't show every extreme that they name: `span_order`: each span number appears once. `doc_starts`: in each row the offsets never fall and the first is 0; document j covers positions from offset j up to offset j + 1, the last up to 1024, so a document may be empty. Among the 1 sequence of each index of dp, one drawn from the seed has its second offset below 64 and all later ones above 960.
All inputs are finite; a program needn't handle non-finite values.
Results may differ from a plain program's by a relative error of at most 0.035.
Values may be sent and summed in bfloat16 or wider, within the bound.
A program may use at most 640 MiB of HBM per device.

v0:
```python
import functools
import math

import jax
import jax.numpy as jnp
import numpy as np
from jax import lax
from jax.experimental import pallas as pl
from jax.experimental.pallas import tpu as pltpu
from jax.sharding import PartitionSpec as P

EPS = 1e-06
NEG = -1e30


def normed(v, gain):
    scale_inv = lax.rsqrt(jnp.mean(v * v, -1, keepdims=True) + EPS)
    return (v * scale_inv * gain, scale_inv)


def norm_back(v, scale_inv, gain, grad):
    scaled = grad * gain
    inner = jnp.mean(scaled * v, -1, keepdims=True)
    dv = scale_inv * scaled - v * scale_inv * scale_inv * scale_inv * inner
    dgain = jnp.sum((grad * v * scale_inv).reshape(-1, v.shape[-1]), 0)
    return (dv, dgain)


def rotary(pos, width):
    half = width // 2
    freqs = jnp.exp(jnp.arange(half, dtype=jnp.float32) * (-2.0 / width * math.log(1000000.0)))
    angle = pos.astype(jnp.float32)[:, None] * freqs[None, :]
    return (jnp.cos(angle)[:, None, :], jnp.sin(angle)[:, None, :])


def rotate(v, cosv, sinv):
    half = v.shape[-1] // 2
    first, second = (v[..., :half], v[..., half:])
    return jnp.concatenate([first * cosv - second * sinv, second * cosv + first * sinv], -1)


def rotate_back(grad, cosv, sinv):
    half = grad.shape[-1] // 2
    first, second = (grad[..., :half], grad[..., half:])
    return jnp.concatenate([first * cosv + second * sinv, second * cosv - first * sinv], -1)


def place(order, begin, count, span):
    rows = begin + jnp.arange(count, dtype=jnp.int32)
    slots = rows // span
    picked = slots[:, None] == jnp.arange(order.shape[0], dtype=jnp.int32)[None, :]
    return jnp.sum(jnp.where(picked, order[None, :], 0), -1) * span + rows % span


def doc_of(starts, pos):
    return jnp.sum((starts[:, None, :] <= pos[None, :, None]).astype(jnp.int32), -1)


def gathered_body(
    tokens,
    out_grad,
    span_order,
    doc_starts,
    w_query,
    w_key,
    w_value,
    w_output,
    attn_gain,
    query_gain,
    key_gain,
    w_gate,
    w_up,
    w_down,
    mlp_gain,
):
    seqs, local, width = tokens.shape
    span = local // 2
    head_size = query_gain.shape[0]
    kv_heads = w_key.shape[1] // head_size
    heads = w_query.shape[1] // head_size
    share = heads // kv_heads
    kv_width = kv_heads * head_size
    ff_width = w_gate.shape[1]
    scale = 1.0 / math.sqrt(head_size)
    total_rows = seqs * local
    own_rows = width // lax.axis_size(("seq", "dp"))
    qpos = place(span_order, lax.axis_index("seq") * local, local, span)
    qdoc = doc_of(doc_starts, qpos)
    cosv, sinv = rotary(qpos, head_size)

    def gather_attn():
        return (
            lax.all_gather(w_query, ("seq", "dp"), axis=0, tiled=True),
            lax.all_gather(w_key, ("seq", "dp"), axis=0, tiled=True),
            lax.all_gather(w_value, ("seq", "dp"), axis=0, tiled=True),
            lax.all_gather(w_output, ("seq", "dp"), axis=0, tiled=True),
            lax.all_gather(
                attn_gain.astype(jnp.bfloat16), ("seq", "dp"), axis=0, tiled=True
            ).astype(attn_gain.dtype),
        )

    def gather_mlp():
        return (
            lax.all_gather(w_gate, ("seq", "dp"), axis=0, tiled=True),
            lax.all_gather(w_up, ("seq", "dp"), axis=0, tiled=True),
            lax.all_gather(w_down, ("seq", "dp"), axis=0, tiled=True),
            lax.all_gather(mlp_gain.astype(jnp.bfloat16), ("seq", "dp"), axis=0, tiled=True).astype(
                mlp_gain.dtype
            ),
        )

    x_rows = tokens.astype(jnp.float32).reshape(total_rows, width)
    wq_all, wk_all, wv_all, wo_all, ga_all = gather_attn()
    first_norm, first_inv = normed(x_rows, ga_all)
    first_in = first_norm.astype(jnp.bfloat16)
    q_raw = jnp.dot(first_in, wq_all, preferred_element_type=jnp.float32).reshape(
        seqs, local, heads, head_size
    )
    k_raw = jnp.dot(first_in, wk_all, preferred_element_type=jnp.float32).reshape(
        seqs, local, kv_heads, head_size
    )
    v_low = (
        jnp.dot(first_in, wv_all, preferred_element_type=jnp.float32)
        .astype(jnp.bfloat16)
        .reshape(seqs, local, kv_heads, head_size)
    )
    q_normed, q_inv = normed(q_raw, query_gain)
    k_normed, k_inv = normed(k_raw, key_gain)
    q_low = rotate(q_normed, cosv, sinv).astype(jnp.bfloat16)
    k_low = rotate(k_normed, cosv, sinv).astype(jnp.bfloat16)
    q_group = q_low.reshape(seqs, local, kv_heads, share, head_size)

    def scores(piece_key, start):
        count = piece_key.shape[1]
        kpos = place(span_order, start, count, span)
        kdoc = doc_of(doc_starts, kpos)
        visible = (qdoc[:, :, None] == kdoc[:, None, :]) & (
            kpos[None, None, :] <= qpos[None, :, None]
        )
        raw = (
            jnp.einsum("sqgjd,skgd->sgjqk", q_group, piece_key, preferred_element_type=jnp.float32)
            * scale
        )
        return (raw, visible[:, None, None])

    start_top = jnp.full((seqs, kv_heads, share, local), NEG, jnp.float32)
    piece = (
        lax.all_gather(k_low, "seq", axis=1, tiled=True),
        lax.all_gather(v_low, "seq", axis=1, tiled=True),
    )
    top = start_top
    raw, visible = scores(piece[0], jnp.int32(0))
    raw = jnp.where(visible, raw, NEG)
    new_top = jnp.maximum(top, jnp.max(raw, -1))
    weights = jnp.where(visible, jnp.exp(raw - new_top[..., None]), 0.0)
    total = jnp.sum(weights, -1)
    summed = jnp.einsum(
        "sgjqk,skgd->sgjqd",
        weights.astype(jnp.bfloat16),
        piece[1],
        preferred_element_type=jnp.float32,
    )
    top, total, summed = (new_top, total, summed)
    log_total = top + jnp.log(total)
    attn_vals = summed / total[..., None]
    out_low = (
        jnp.transpose(attn_vals, (0, 3, 1, 2, 4))
        .reshape(total_rows, heads * head_size)
        .astype(jnp.bfloat16)
    )
    resid = x_rows + jnp.einsum("nh,dh->nd", out_low, wo_all, preferred_element_type=jnp.float32)
    wg_all, wu_all, wd_all, gm_all = gather_mlp()
    second_norm, second_inv = normed(resid, gm_all)
    second_in = second_norm.astype(jnp.bfloat16)
    gate = jnp.dot(second_in, wg_all, preferred_element_type=jnp.float32)
    upper = jnp.dot(second_in, wu_all, preferred_element_type=jnp.float32)
    sigma = jax.nn.sigmoid(gate)
    act = gate * sigma
    hidden = (act * upper).astype(jnp.bfloat16)
    result = resid + jnp.einsum("nf,df->nd", hidden, wd_all, preferred_element_type=jnp.float32)
    block_out = result.astype(jnp.bfloat16).reshape(seqs, local, width)
    grad_low = out_grad.reshape(total_rows, width)
    wg_all, wu_all, wd_all, gm_all = gather_mlp()
    dmid = jnp.einsum("nd,df->nf", grad_low, wd_all, preferred_element_type=jnp.float32)
    dgate = (dmid * upper * sigma * (1.0 + gate * (1.0 - sigma))).astype(jnp.bfloat16)
    dupper = (dmid * act).astype(jnp.bfloat16)
    left = second_in
    outer = grad_low
    mlp_sums = lax.psum_scatter(
        jnp.concatenate(
            [
                jnp.einsum("nd,nf->df", left, dgate, preferred_element_type=jnp.float32),
                jnp.einsum("nd,nf->df", left, dupper, preferred_element_type=jnp.float32),
                jnp.einsum("nd,nf->df", outer, hidden, preferred_element_type=jnp.float32),
            ],
            1,
        ),
        ("seq", "dp"),
        scatter_dimension=0,
        tiled=True,
    )
    dsecond = jnp.einsum(
        "nf,df->nd", dgate, wg_all, preferred_element_type=jnp.float32
    ) + jnp.einsum("nf,df->nd", dupper, wu_all, preferred_element_type=jnp.float32)
    dresid_norm, dgm = norm_back(resid, second_inv, gm_all, dsecond)
    dresid = grad_low.astype(jnp.float32) + dresid_norm
    dresid_low = dresid.astype(jnp.bfloat16)
    wq_all, wk_all, wv_all, wo_all, ga_all = gather_attn()
    dout_low = jnp.einsum(
        "nd,dh->nh", dresid_low, wo_all, preferred_element_type=jnp.float32
    ).astype(jnp.bfloat16)
    dout_group = dout_low.reshape(seqs, local, kv_heads, share, head_size)
    delta = jnp.sum(jnp.transpose(dout_group.astype(jnp.float32), (0, 2, 3, 1, 4)) * attn_vals, -1)
    piece = (
        lax.all_gather(k_low, "seq", axis=1, tiled=True),
        lax.all_gather(v_low, "seq", axis=1, tiled=True),
    )
    count = piece[0].shape[1]
    raw, visible = scores(piece[0], jnp.int32(0))
    prob = jnp.where(visible, jnp.exp(raw - log_total[..., None]), 0.0)
    dprob = jnp.einsum(
        "sqgjd,skgd->sgjqk", dout_group, piece[1], preferred_element_type=jnp.float32
    )
    dscore = (prob * (dprob - delta[..., None])).astype(jnp.bfloat16)
    dq_sum = jnp.einsum("sgjqk,skgd->sqgjd", dscore, piece[0], preferred_element_type=jnp.float32)
    dk_part = (
        jnp.einsum("sgjqk,sqgjd->skgd", dscore, q_group, preferred_element_type=jnp.float32) * scale
    )
    dv_part = jnp.einsum(
        "sgjqk,sqgjd->skgd",
        prob.astype(jnp.bfloat16),
        dout_group,
        preferred_element_type=jnp.float32,
    )
    joined = jnp.concatenate(
        [dk_part.reshape(seqs, count, kv_width), dv_part.reshape(seqs, count, kv_width)], -1
    )
    buffer = joined
    dq_sum, buffer = (dq_sum, buffer)
    key_sums = lax.psum_scatter(
        buffer.astype(jnp.bfloat16), "seq", scatter_dimension=1, tiled=True
    ).astype(jnp.float32)
    dq_rot = (dq_sum * scale).reshape(seqs, local, heads, head_size)
    dq_raw, dgq = norm_back(q_raw, q_inv, query_gain, rotate_back(dq_rot, cosv, sinv))
    dk_rot = key_sums[..., :kv_width].reshape(seqs, local, kv_heads, head_size)
    dk_raw, dgk = norm_back(k_raw, k_inv, key_gain, rotate_back(dk_rot, cosv, sinv))
    dq_low = dq_raw.reshape(total_rows, heads * head_size).astype(jnp.bfloat16)
    dk_low = dk_raw.reshape(total_rows, kv_width).astype(jnp.bfloat16)
    dv_low = key_sums[..., kv_width:].reshape(total_rows, kv_width).astype(jnp.bfloat16)
    left = first_in
    outer = dresid_low
    attn_sums = lax.psum_scatter(
        jnp.concatenate(
            [
                jnp.einsum("nd,nh->dh", left, dq_low, preferred_element_type=jnp.float32),
                jnp.einsum("nd,nh->dh", left, dk_low, preferred_element_type=jnp.float32),
                jnp.einsum("nd,nh->dh", left, dv_low, preferred_element_type=jnp.float32),
                jnp.einsum("nd,nh->dh", outer, out_low, preferred_element_type=jnp.float32),
            ],
            1,
        ),
        ("seq", "dp"),
        scatter_dimension=0,
        tiled=True,
    )
    dfirst = jnp.einsum("nh,dh->nd", dq_low, wq_all, preferred_element_type=jnp.float32)
    dfirst = dfirst + jnp.einsum("nh,dh->nd", dk_low, wk_all, preferred_element_type=jnp.float32)
    dfirst = dfirst + jnp.einsum("nh,dh->nd", dv_low, wv_all, preferred_element_type=jnp.float32)
    dx_norm, dga = norm_back(x_rows, first_inv, ga_all, dfirst)
    tokens_grad = (dresid + dx_norm).reshape(seqs, local, width)
    dga_all, dgm_all, dgq_all, dgk_all = lax.psum((dga, dgm, dgq, dgk), ("seq", "dp"))
    offset = lax.axis_index(("seq", "dp")) * own_rows
    attn_gain_grad = lax.dynamic_slice_in_dim(dga_all, offset, own_rows, 0)
    mlp_gain_grad = lax.dynamic_slice_in_dim(dgm_all, offset, own_rows, 0)
    q_cols = heads * head_size
    w_query_grad = attn_sums[:, :q_cols]
    w_key_grad = attn_sums[:, q_cols : q_cols + kv_width]
    w_value_grad = attn_sums[:, q_cols + kv_width : q_cols + 2 * kv_width]
    w_output_grad = attn_sums[:, q_cols + 2 * kv_width :]
    w_gate_grad = mlp_sums[:, :ff_width]
    w_up_grad = mlp_sums[:, ff_width : 2 * ff_width]
    w_down_grad = mlp_sums[:, 2 * ff_width :]
    return (
        block_out,
        tokens_grad,
        w_query_grad,
        w_key_grad,
        w_value_grad,
        w_output_grad,
        attn_gain_grad,
        dgq_all,
        dgk_all,
        w_gate_grad,
        w_up_grad,
        w_down_grad,
        mlp_gain_grad,
    )


LOW = jnp.bfloat16
MESH = pl.DeviceIdType.MESH
LIMIT = 60 * 2**20


def ring_order(ranks):
    half = ranks // 2
    order = [0]
    for step in range(1, half):
        order += [step, ranks - step]
    return order + [half]


def ring_place(seq, ranks):
    z, x = lax.div(seq, 2), lax.rem(seq, 2)
    return z + x * (ranks - 1 - 2 * z)


def ring_seq(place, ranks):
    half = ranks // 2
    x, z = lax.div(place, half), lax.rem(place, half)
    return 2 * (z + x * (half - 1 - 2 * z)) + x


def neighbours(ranks):
    seq, dp = lax.axis_index("seq"), lax.axis_index("dp")
    at = ring_place(seq, ranks)
    right = ring_seq(lax.rem(at + 1, ranks), ranks)
    left = ring_seq(lax.rem(at + ranks - 1, ranks), ranks)
    return (right, dp), (left, dp)


def knock(devices):
    barrier = pltpu.get_barrier_semaphore()
    for device in devices:
        pl.semaphore_signal(barrier, inc=1, device_id=device, device_id_type=MESH)


def answered(devices):
    pl.semaphore_wait(pltpu.get_barrier_semaphore(), len(devices))


def move(src, dst, sem):
    copy = pltpu.make_async_copy(src, dst, sem)
    copy.start()
    return copy


def push(src, dst, send, recv, device):
    return pltpu.make_async_remote_copy(
        src_ref=src, dst_ref=dst, send_sem=send, recv_sem=recv, device_id=device, device_id_type=MESH
    )


def dot_nn(left, right):
    return jnp.dot(left, right, preferred_element_type=jnp.float32)


def dot_nt(left, right):
    return lax.dot_general(left, right, (((1,), (1,)), ((), ())), preferred_element_type=jnp.float32)


def dot_tn(left, right):
    return lax.dot_general(left, right, (((0,), (0,)), ((), ())), preferred_element_type=jnp.float32)


def block_row(rel, local, ranks):
    place = ring_place(lax.axis_index("seq"), ranks)
    return pl.multiple_of(ring_seq(lax.rem(place + rel, ranks), ranks) * local, local)


def block_rows(ref, rels, local, ranks):
    blocks = [ref[pl.ds(block_row(rel, local, ranks), local)] for rel in rels]
    return blocks[0] if len(blocks) == 1 else jnp.concatenate(blocks, 0)


def rels_of(step, ranks):
    return [rel for rel in ring_order(ranks) if min(rel, ranks - rel) == step]


class RingGather:
    def __init__(self, buf, local, ranks, send, recv, right, left, row):
        self.buf, self.sub, self.half = buf, local // 2, ranks // 2
        self.send, self.recv, self.right, self.left = send, recv, right, left
        self.ranks, self.row = ranks, row

    def copies(self, step, part):
        ways = ((0, (self.ranks - step + 1) % self.ranks, self.right), (1, step - 1, self.left))
        given = []
        for way, rel, device in ways:
            if step < self.half or way == part:
                block = self.buf.at[pl.ds(self.row(rel) + part * self.sub, self.sub)]
                at = 2 * (step - 1) + part
                given.append(push(block, block, self.send.at[way, at], self.recv.at[way, at], device))
        return given

    def start(self, step):
        for part in range(2):
            for copy in self.copies(step, part):
                copy.start()

    def advance(self, step):
        for part in range(2):
            for copy in self.copies(step, part):
                copy.wait_recv()
            if step < self.half:
                for copy in self.copies(step + 1, part):
                    copy.start()

    def finish(self):
        for step in range(1, self.half + 1):
            for part in range(2):
                for copy in self.copies(step, part):
                    copy.wait_send()


class LineGather:
    def __init__(self, buf, local, ranks, send, recv, x_send, x_recv):
        self.buf, self.local, self.length = buf, local, ranks // 2
        self.send, self.recv, self.x_send, self.x_recv = send, recv, x_send, x_recv
        self.seq, self.dp = lax.axis_index("seq"), lax.axis_index("dp")
        self.z, self.x = lax.div(self.seq, 2), lax.rem(self.seq, 2)

    def block(self, z):
        return self.buf.at[pl.ds(pl.multiple_of((2 * z + self.x) * self.local, self.local), self.local)]

    def hop(self, way, step):
        block = self.block(self.z + (step - 1 if way else 1 - step))
        to = self.seq + (-2 if way else 2)
        return push(block, block, self.send.at[way, step - 1], self.recv.at[way, step - 1], (to, self.dp))

    def sends(self, way, step):
        if way:
            return (self.z > 0) & (self.z + step <= self.length)
        return (self.z < self.length - 1) & (self.z >= step - 1)

    def comes(self, way, step):
        return self.z + step < self.length if way else self.z >= step

    def across(self, way, step):
        block = self.block(self.z + (step if way else -step))
        at = step + way * (self.length - 1)
        return push(
            block, block, self.x_send.at[at], self.x_recv.at[at], (self.seq + 1 - 2 * self.x, self.dp)
        )

    def from_x(self, way, step):
        z = self.z + (step if way else -step)
        row = pl.multiple_of((2 * z + 1 - self.x) * self.local, self.local)
        block = self.buf.at[pl.ds(row, self.local)]
        at = step + way * (self.length - 1)
        return push(
            block, block, self.x_send.at[at], self.x_recv.at[at], (self.seq + 1 - 2 * self.x, self.dp)
        )

    def start(self, step):
        for way in range(2):
            pl.when(self.sends(way, step))(lambda way=way: self.hop(way, step).start())
        self.pass_on(step - 1)

    def pass_on(self, step):
        if step == 0:
            self.across(0, 0).start()
            return
        for way in range(2):
            pl.when(self.comes(way, step))(lambda way=way: self.across(way, step).start())

    def arrive(self, step):
        for way in range(2):
            pl.when(self.comes(way, step))(lambda way=way: self.incoming(way, step).wait_recv())

    def incoming(self, way, step):
        block = self.block(self.z + (step if way else -step))
        to = self.seq + 1 - 2 * self.x
        return push(block, block, self.send.at[way, step - 1], self.recv.at[way, step - 1], (to, self.dp))

    def run(self):
        for step in range(1, self.length):
            self.advance(step)

    def advance(self, step):
        self.arrive(step)
        if step < self.length - 1:
            self.start(step + 1)
        else:
            self.pass_on(step)

    def complete(self):
        self.from_x(0, 0).wait_recv()
        for step in range(1, self.length):
            for way in range(2):
                pl.when(self.comes(way, step))(lambda way=way: self.from_x(way, step).wait_recv())

    def finish(self):
        self.across(0, 0).wait_send()
        for step in range(1, self.length):
            for way in range(2):
                pl.when(self.sends(way, step))(lambda way=way: self.hop(way, step).wait_send())
                pl.when(self.comes(way, step))(lambda way=way: self.across(way, step).wait_send())


def line_sems(ranks):
    half = ranks // 2
    return [pltpu.SemaphoreType.DMA((2, half))] * 2 + [pltpu.SemaphoreType.DMA((2 * half,))] * 2


class RingSum:
    def __init__(self, part, term, out_buf, in_buf, local, ranks, send, recv, right, left, stream=0, streams=1):
        self.part, self.term, self.out_buf, self.in_buf = part, term, out_buf, in_buf
        self.local, self.ranks, self.half = local, ranks, ranks // 2
        each = term.shape[1] // streams
        self.cols = pl.ds(stream * each, each)
        self.tiles = (stream * ranks // streams, (stream + 1) * ranks // streams)
        self.send, self.recv, self.right, self.left = send, recv, right, left

    def copies(self, step):
        rows = self.local // 2 if step == 1 else self.local
        skip = self.local // 2 if step == 1 else 0
        return [
            push(
                self.out_buf.at[way, (step - 1) % 2, pl.ds(begin, rows), self.cols],
                self.in_buf.at[way, step - 1, pl.ds(begin, rows), self.cols],
                self.send.at[way, step - 1],
                self.recv.at[way, step - 1],
                device,
            )
            for way, begin, device in ((0, 0, self.right), (1, skip, self.left))
        ]

    def compute(self, step):
        if step == 1:
            self.part([self.half], *self.tiles)
        elif step <= self.half:
            self.part(rels_of(self.half + 1 - step, self.ranks), *self.tiles)
        else:
            self.part([0], *self.tiles)

    def launch(self, step):
        local, skip = self.local, self.local // 2
        if step > 2:
            for copy in self.copies(step - 2):
                copy.wait_send()
        if step == 1:
            for way in range(2):
                rows = pl.ds(way * skip, skip)
                self.out_buf[way, 0, rows, self.cols] = self.term[rows, self.cols].astype(LOW)
        else:
            for copy in self.copies(step - 1):
                copy.wait_recv()
            for way in range(2):
                for begin, with_sum in ((0, step > 2 or way == 0), (skip, step > 2 or way == 1)):
                    value = self.term[pl.ds(way * local + begin, skip), self.cols]
                    if with_sum:
                        value = value + self.in_buf[way, step - 2, pl.ds(begin, skip), self.cols].astype(jnp.float32)
                    self.out_buf[way, (step - 1) % 2, pl.ds(begin, skip), self.cols] = value.astype(LOW)
        for copy in self.copies(step):
            copy.start()

    def last(self, begin, count):
        rows = pl.ds(begin, count)
        value = self.term[rows, self.cols] + self.in_buf[0, self.half - 1, rows, self.cols].astype(jnp.float32)
        return value + self.in_buf[1, self.half - 1, rows, self.cols].astype(jnp.float32)

    def arrive_last(self):
        for copy in self.copies(self.half):
            copy.wait_recv()

    def finish(self):
        for step in range(max(1, self.half - 1), self.half + 1):
            for copy in self.copies(step):
                copy.wait_send()


def two_sums(part, term, out_buf, in_buf, local, ranks, sems, right, left):
    return [
        RingSum(
            part, term, out_buf, in_buf, local, ranks, sems[2 * at], sems[2 * at + 1], right, left, at, 2
        )
        for at in range(2)
    ]


def ring_sems(ranks):
    return [pltpu.SemaphoreType.DMA((2, ranks)), pltpu.SemaphoreType.DMA((2, ranks))]


def sum_bufs(local, ranks, width):
    return [
        pltpu.VMEM((2 * local, width), jnp.float32),
        pltpu.VMEM((2, 2, local, width), LOW),
        pltpu.VMEM((2, ranks // 2, local, width), LOW),
    ]


def turn(v):
    return pltpu.roll(v, v.shape[-1] // 2, v.ndim - 1)


def rows_scaled(v):
    inv = lax.rsqrt(jnp.mean(v * v, -1, keepdims=True) + EPS)
    return v * inv, inv


def rows_scaled_back(v, inv, grad):
    return inv * grad - v * (inv * inv * inv * jnp.mean(grad * v, -1, keepdims=True))


class Spread:
    def __init__(self, rows, block, ranks, own, cols, sems):
        self.rows, self.block, self.ranks, self.own, self.cols = rows, block, ranks, own, cols
        self.send, self.recv, self.hop_send, self.hop_recv, self.here = sems
        self.seq, self.dp = lax.axis_index("seq"), lax.axis_index("dp")
        y, core = lax.div(self.dp, 2), lax.rem(self.dp, 2)
        self.beside, self.sibling = (1 - y) * 2 + core, y * 2 + 1 - core

    def at(self, dp):
        return pl.ds(pl.multiple_of(dp * self.own, self.own), self.own)

    def exchange(self):
        for step in range(1, self.ranks):
            peer = lax.rem(self.seq + step, self.ranks)
            yield push(
                self.rows.at[peer, :, self.cols],
                self.block.at[self.seq, self.at(self.dp), self.cols],
                self.send.at[step],
                self.recv.at[step],
                (peer, self.dp),
            )

    def keep(self):
        return pltpu.make_async_copy(
            self.rows.at[self.seq, :, self.cols],
            self.block.at[self.seq, self.at(self.dp), self.cols],
            self.here,
        )

    def hop(self, number):
        dp = self.beside if number == 2 else self.dp
        part = self.block.at[:, self.at(dp), self.cols]
        to = self.beside if number == 0 else self.sibling
        return push(part, part, self.hop_send.at[number], self.hop_recv.at[number], (self.seq, to))

    def start(self):
        self.keep().start()
        for copy in self.exchange():
            copy.start()

    def arrive(self):
        self.keep().wait()
        for copy in self.exchange():
            copy.wait_recv()

    def finish(self):
        for copy in self.exchange():
            copy.wait_send()
        for number in range(3):
            self.hop(number).wait_send()


def spread_sems(ranks):
    return [
        pltpu.SemaphoreType.DMA((ranks,)),
        pltpu.SemaphoreType.DMA((ranks,)),
        pltpu.SemaphoreType.DMA((3,)),
        pltpu.SemaphoreType.DMA((3,)),
        pltpu.SemaphoreType.DMA,
    ]


class WholeGather:
    def __init__(self, block, ranks, own, sems):
        self.block, self.ranks, self.half, self.own = block, ranks, ranks // 2, own
        self.send, self.recv, self.y_send, self.y_recv, self.core_send, self.core_recv = sems
        self.seq, self.dp = lax.axis_index("seq"), lax.axis_index("dp")
        self.right, self.left = neighbours(ranks)
        self.place = ring_place(self.seq, ranks)
        y, core = lax.div(self.dp, 2), lax.rem(self.dp, 2)
        self.beside, self.sibling = (1 - y) * 2 + core, y * 2 + 1 - core

    def at(self, rel, dp, begin, count):
        seq = ring_seq(lax.rem(self.place + rel + self.ranks, self.ranks), self.ranks)
        return self.block.at[seq, pl.ds(pl.multiple_of(dp * self.own + begin, count), count)]

    def copies(self, step):
        last = step == self.half
        rows = self.own // 2 if last else self.own
        skip = self.own // 2 if last else 0
        given = []
        for way, rel, begin, device in ((0, 1 - step, 0, self.right), (1, step - 1, skip, self.left)):
            part = self.at(rel, self.dp, begin, rows)
            given.append(push(part, part, self.send.at[way, step - 1], self.recv.at[way, step - 1], device))
        return given

    def start(self, step):
        for copy in self.copies(step):
            copy.start()

    def hops(self, step):
        for at, rel in enumerate(ring_order(self.ranks)):
            if min(rel, self.ranks - rel) == step:
                part = self.at(rel, self.dp, 0, self.own)
                yield push(part, part, self.y_send.at[at], self.y_recv.at[at], (self.seq, self.beside))
                yield push(part, part, self.core_send.at[at], self.core_recv.at[at], (self.seq, self.sibling))

    def arrive(self, step):
        for copy in self.copies(step):
            copy.wait_recv()

    def forward(self, step):
        for copy in self.hops(step):
            copy.start()

    def cross(self):
        part = self.block.at[:, pl.ds(pl.multiple_of(self.beside * self.own, self.own), self.own)]
        at = self.ranks
        return push(part, part, self.core_send.at[at], self.core_recv.at[at], (self.seq, self.sibling))

    def complete(self):
        for step in range(self.half + 1):
            for copy in self.hops(step):
                copy.wait_recv()
        self.cross().start()
        self.cross().wait_recv()

    def finish(self):
        for step in range(1, self.half + 1):
            for copy in self.copies(step):
                copy.wait_send()
        for step in range(self.half + 1):
            for copy in self.hops(step):
                copy.wait_send()
        self.cross().wait_send()


def whole_sems(ranks):
    return (
        ring_sems(ranks)
        + [pltpu.SemaphoreType.DMA((ranks,))] * 2
        + [pltpu.SemaphoreType.DMA((ranks + 1,))] * 2
    )


class Reduce:
    def __init__(self, grads, from_core, from_y, total, own, first, count, cols, sems):
        self.grads, self.from_core, self.from_y, self.total = grads, from_core, from_y, total
        self.own, self.begin, self.count, self.cols = own, first, count, cols
        self.send, self.recv = sems
        self.seq, dp = lax.axis_index("seq"), lax.axis_index("dp")
        self.y, self.core = lax.div(dp, 2), lax.rem(dp, 2)
        self.beside, self.sibling = (1 - self.y) * 2 + self.core, self.y * 2 + 1 - self.core

    def at(self, y, core):
        return pl.ds(pl.multiple_of((y * 2 + core) * self.own, self.own), self.own)

    def hop(self, number):
        some, cols = pl.ds(self.begin, self.count), self.cols
        if number == 2:
            src, dst, to = self.from_core.at[0, some, :, cols], self.from_y.at[some, :, cols], self.beside
        else:
            rows = self.at(1 - self.y if number == 0 else self.y, 1 - self.core)
            src, dst, to = self.grads.at[some, rows, cols], self.from_core.at[number, some, :, cols], self.sibling
        return push(src, dst, self.send.at[number], self.recv.at[number], (self.seq, to))

    def first(self):
        self.hop(0).start()
        self.hop(1).start()

    def second(self):
        self.hop(0).wait_recv()
        rows = self.at(1 - self.y, self.core)

        def some(at, _):
            value = self.grads[at, rows, self.cols].astype(jnp.float32)
            value = value + self.from_core[0, at, :, self.cols].astype(jnp.float32)
            self.from_core[0, at, :, self.cols] = value.astype(LOW)
            return 0

        lax.fori_loop(self.begin, self.begin + self.count, some, 0)
        self.hop(2).start()

    def third(self):
        self.hop(1).wait_recv()
        self.hop(2).wait_recv()
        rows = self.at(self.y, self.core)

        def some(at, _):
            value = self.grads[at, rows, self.cols].astype(jnp.float32)
            value = value + self.from_core[1, at, :, self.cols].astype(jnp.float32)
            value = value + self.from_y[at, :, self.cols].astype(jnp.float32)
            self.total[at, :, self.cols] = value.astype(LOW)
            return 0

        lax.fori_loop(self.begin, self.begin + self.count, some, 0)

    def finish(self):
        for number in range(3):
            self.hop(number).wait_send()


def reduce_sems():
    return [pltpu.SemaphoreType.DMA((3,)), pltpu.SemaphoreType.DMA((3,))]


def reduce_bufs(ranks, own, cols):
    return [pltpu.VMEM((2, ranks, own, cols), LOW), pltpu.VMEM((ranks, own, cols), LOW)]


class Deliver:
    def __init__(self, rows, out, cols, ranks, sems):
        self.rows, self.out, self.cols, self.ranks = rows, out, cols, ranks
        self.send, self.recv, self.here = sems
        self.seq, self.dp = lax.axis_index("seq"), lax.axis_index("dp")

    def exchange(self):
        for step in range(1, self.ranks):
            peer = lax.rem(self.seq + step, self.ranks)
            yield push(
                self.rows.at[peer, :, self.cols],
                self.out.at[self.seq, :, self.cols],
                self.send.at[step],
                self.recv.at[step],
                (peer, self.dp),
            )

    def keep(self):
        return pltpu.make_async_copy(
            self.rows.at[self.seq, :, self.cols], self.out.at[self.seq, :, self.cols], self.here
        )

    def start(self):
        self.keep().start()
        for copy in self.exchange():
            copy.start()

    def finish(self):
        self.keep().wait()
        for copy in self.exchange():
            copy.wait_recv()
        for copy in self.exchange():
            copy.wait_send()


def deliver_sems(ranks):
    return [pltpu.SemaphoreType.DMA((ranks,)), pltpu.SemaphoreType.DMA((ranks,)), pltpu.SemaphoreType.DMA]


def first_kernel(
    ranks, kv_heads, order, starts, tokens, out_grad, freqs, attn_gain, mlp_gain, query_gain, key_gain,
    w_query, w_key, w_value, w_output, w_gate, w_up, w_down,
    resid, second, cosv, sinv, q_low, k_low, v_low, own_out, first_in, qkv, attn_block, dy_all, prob, mlp_block, out_all,
    held, normal, kept, block, a_rows, m_rows, gate, up, down, dys, probs, pos, begins, pos_row,
    out_low, whole, *sems,
):
    local, width = tokens.shape
    rows = local * ranks
    own = w_query.shape[0]
    size = freqs.shape[1]
    heads = q_low.shape[0]
    share = heads // kv_heads
    half = ranks // 2
    scale = 1.0 / math.sqrt(size)
    cols = (heads + 2 * kv_heads) * size
    deep = block.shape[1]
    row = functools.partial(block_row, local=local, ranks=ranks)
    seq, dp = lax.axis_index("seq"), lax.axis_index("dp")
    right, left = neighbours(ranks)
    attn = Spread(a_rows, block, ranks, own, pl.ds(0, a_rows.shape[2]), sems[12:17])
    third = m_rows.shape[2] // 3
    mlp = [
        Spread(m_rows, mlp_block, ranks, own, pl.ds(at * third, third), sems[17 + 5 * at : 22 + 5 * at])
        for at in range(3)
    ]
    local_sems = sems[32]
    out_send, out_recv = sems[2:4]
    o_cols = heads * size
    peers = [(lax.rem(seq + step, ranks), dp) for step in range(1, ranks)]
    peers += [(seq, attn.beside), (seq, attn.sibling)]
    knock(peers)
    loads = [
        move(src, dst, local_sems.at[at])
        for at, (src, dst) in enumerate(((w_gate, gate), (w_up, up), (w_down, down)))
    ]
    held[pl.ds(row(0), local)] = tokens[...]
    dys[pl.ds(row(0), local)] = out_grad[...]

    def column(line):
        same = lax.broadcasted_iota(jnp.int32, (own, own), 0) == lax.broadcasted_iota(jnp.int32, (own, own), 1)
        return jnp.sum(jnp.where(same, line, 0.0), 1, keepdims=True)

    def lay(target, begin, weight, gain):
        each = weight.shape[1] // ranks
        for rank in range(ranks):
            part = weight[:, rank * each : (rank + 1) * each]
            if gain is not None:
                part = (part.astype(jnp.float32) * gain).astype(LOW)
            target[rank, :, begin : begin + each] = part
        return begin + each

    gain = column(attn_gain[...])
    at = 0
    for weight in (w_query, w_key, w_value):
        at = lay(a_rows, at, weight, gain)
    whole[seq, pl.ds(pl.multiple_of(dp * own, own), own)] = w_output[...]
    answered(peers)
    ring = RingGather(held, local, ranks, sems[0], sems[1], right, left, row)
    ring.start(1)
    attn.start()
    outs = WholeGather(whole, ranks, own, [*sems[8:12], *sems[33:35]])
    outs.forward(0)
    line = LineGather(dys, local, ranks, sems[4], sems[5], sems[6], sems[7])
    stores = []

    def store(src, dst):
        stores.append(move(src, dst, local_sems.at[len(loads) + len(stores)]))

    def scale_rows(step):
        for rel in rels_of(step, ranks):

            def some(at, _):
                rows_at = pl.ds(pl.multiple_of(row(rel) + at * 32, 32), 32)
                normal[rows_at] = rows_scaled(held[rows_at].astype(jnp.float32))[0].astype(LOW)
                return 0

            lax.fori_loop(0, local // 32, some, 0)

    for load in loads:
        load.wait()
    gain = column(mlp_gain[...])
    each = gate.shape[1] // ranks
    lay(m_rows, 0, gate, gain)
    lay(m_rows, each, up, gain)
    lay(m_rows, 2 * each, down, None)
    scale_rows(0)
    def bring(step):
        outs.arrive(step)
        if step < half:
            outs.start(step + 1)
        outs.forward(step)

    def forward(piece):
        mlp[piece].arrive()
        mlp[piece].hop(0).start()
        mlp[piece].hop(1).start()

    def hop_over(piece):
        mlp[piece].hop(0).wait_recv()
        mlp[piece].hop(2).start()

    def pass_on(step):
        ring.advance(step)
        scale_rows(step)

    pass_on(1)
    line.start(1)
    pass_on(2)
    outs.start(1)
    attn.arrive()
    attn.hop(0).start()
    attn.hop(1).start()
    attn.hop(0).wait_recv()
    attn.hop(2).start()
    for step in range(3, half):
        pass_on(step)
    bring(1)
    pass_on(half)
    mlp[0].start()
    spans = order.shape[0]
    span = rows // spans
    for at in range(ranks):
        rows_at = pl.ds(at * local, local)
        ids = at * local + lax.broadcasted_iota(jnp.int32, (1, local), 1)
        where = jnp.zeros_like(ids)
        for slot in range(spans):
            inside = (ids >= slot * span) & (ids < (slot + 1) * span)
            where = where + jnp.where(inside, ids + (order[slot] - slot) * span, 0)
        begin = jnp.zeros_like(ids)
        for doc in range(starts.shape[1]):
            begin = jnp.maximum(begin, jnp.where(starts[0, doc] <= where, starts[0, doc], 0))
        pos_row[:, rows_at] = where
        across = jnp.broadcast_to(where, (local, local)).T
        pos[rows_at] = across[:, :1]
        begins[rows_at] = jnp.broadcast_to(begin, (local, local)).T[:, :1]
        angle = across[:, :1].astype(jnp.float32) * freqs[...]
        lane = lax.broadcasted_iota(jnp.int32, (local, size), 1)
        cosv[rows_at] = jnp.cos(angle)
        sine = jnp.sin(angle)
        sinv[rows_at] = jnp.where(lane < size // 2, -sine, sine)
    bring(2)
    line.advance(1)
    attn.hop(1).wait_recv()
    attn.hop(2).wait_recv()
    store(block, attn_block)

    def project(begin, count):
        rows_at = pl.ds(begin, count)
        kept[rows_at] = dot_nn(normal[rows_at], block[...].reshape(width, cols))

    store(normal, first_in)
    tile = rows // half

    def rotated(at, rows_at, gain):
        v = rows_scaled(kept[rows_at, at * size : (at + 1) * size])[0] * gain[...]
        return (v * cosv[rows_at] + turn(v) * sinv[rows_at]).astype(LOW)

    for piece in range(half):
        rows_at = pl.ds(piece * tile, tile)
        project(piece * tile, tile)
        for head in range(heads):
            q_low[head, rows_at] = rotated(head, rows_at, query_gain)
        for group in range(kv_heads):
            k_low[group, rows_at] = rotated(heads + group, rows_at, key_gain)
            at = (heads + kv_heads + group) * size
            v_low[group, rows_at] = kept[rows_at, at : at + size].astype(LOW)
    store(kept, qkv)
    forward(0)

    for piece in range(half):
        rows_at = pl.ds(piece * tile, tile)
        seen = (pos_row[...] <= pos[rows_at]) & (pos_row[...] >= begins[rows_at])
        for head in range(heads):
            raw = dot_nt(q_low[head, rows_at], k_low[head // share]) * scale
            raw = jnp.where(seen, raw, NEG)
            weight = jnp.exp(raw - jnp.max(raw, -1, keepdims=True))
            weight = (weight * (1.0 / jnp.sum(weight, -1, keepdims=True))).astype(LOW)
            probs[head, rows_at] = weight
            value = dot_nn(weight, v_low[head // share])
            out_low[rows_at, head * size : (head + 1) * size] = value.astype(LOW)
            store(probs.at[head, rows_at], prob.at[head, rows_at])
        if piece == 0:
            bring(3)
        if piece == 1:
            mlp[1].start()
            line.advance(2)
            bring(half)
    mlp[2].start()
    hop_over(0)
    forward(1)
    forward(2)
    place = ring_place(seq, ranks)

    def exchange(rel):
        to = ring_seq(lax.rem(place + rel, ranks), ranks)
        return push(
            out_low.at[pl.ds(row(rel), local)],
            own_out.at[:, pl.ds(pl.multiple_of(seq * o_cols, o_cols), o_cols)],
            out_send.at[rel],
            out_recv.at[rel],
            (to, dp),
        )

    for rel in range(1, ranks):
        exchange(rel).start()
    own_out[:, pl.ds(pl.multiple_of(seq * o_cols, o_cols), o_cols)] = out_low[pl.ds(row(0), local)]
    outs.complete()
    store(whole, out_all)
    hop_over(1)
    for step in range(3, half):
        line.advance(step)
    for rel in range(1, ranks):
        exchange(rel).wait_recv()

    def join(at, _):
        some = pl.ds(pl.multiple_of(at * deep, deep), deep)
        resid[:, some] = tokens[:, some].astype(jnp.float32) + dot_nt(own_out[...], whole[at])
        return 0

    lax.fori_loop(0, ranks, join, 0)

    def scale_second(at, _):
        rows_at = pl.ds(pl.multiple_of(at * 32, 32), 32)
        second[rows_at] = rows_scaled(resid[rows_at])[0].astype(LOW)
        return 0

    lax.fori_loop(0, local // 32, scale_second, 0)
    hop_over(2)
    line.complete()
    store(dys, dy_all)
    ring.finish()
    attn.finish()
    outs.finish()
    for rel in range(1, ranks):
        exchange(rel).wait_send()
    line.finish()
    for piece in mlp:
        piece.hop(1).wait_recv()
        piece.hop(2).wait_recv()
        piece.finish()
    for given in stores:
        given.wait()


def mlp_kernel(
    ranks, second, out_grad, rest, dys, mlp_block, block_out, dresid, dresid_low, own_grads,
    grads, from_core, from_y, held, weights, hidden, dgu, resid, dy_all,
    term, out_buf, in_buf, y_out, y_in, here, *sems,
):
    local, width = second.shape
    row = functools.partial(block_row, local=local, ranks=ranks)
    ff = hidden.shape[1]
    deep = weights.shape[1]
    half = ranks // 2
    right, left = neighbours(ranks)
    loads = [
        move(src, dst, here.at[at])
        for at, (src, dst) in enumerate(((mlp_block, weights), (dys, dy_all), (rest, resid)))
    ]
    seq, dp = lax.axis_index("seq"), lax.axis_index("dp")
    own = own_grads.shape[1]
    pieces = [
        Reduce(
            grads, from_core, from_y, own_grads, own, at * ranks // 4, ranks // 4, pl.ds(0, 3 * ff),
            sems[6 + 2 * at : 8 + 2 * at],
        )
        for at in range(4)
    ]
    peers = [right, left, (seq, pieces[0].beside), (seq, pieces[0].sibling)]
    knock(peers)
    held[pl.ds(row(0), local)] = second[...]
    answered(peers)
    ring = RingGather(held, local, ranks, sems[0], sems[1], right, left, row)
    ring.start(1)
    loads[0].wait()
    loads[1].wait()
    wide = 256

    def middle(step):
        rels = rels_of(step, ranks)

        def some(at, _):
            first = pl.multiple_of(at * wide, wide)
            given, dy = block_rows(held, rels, local, ranks), block_rows(dy_all, rels, local, ranks)
            gate = dot_nn(given, weights[:, :, pl.ds(first, wide)].reshape(width, wide))
            upper = dot_nn(given, weights[:, :, pl.ds(ff + first, wide)].reshape(width, wide))
            dmid = dot_nn(dy, weights[:, :, pl.ds(2 * ff + first, wide)].reshape(width, wide))
            sigma = 1.0 / (1.0 + jnp.exp(-gate))
            act = gate * sigma
            value = (act * upper).astype(LOW)
            dgate = (dmid * upper * (sigma * (1.0 + gate * (1.0 - sigma)))).astype(LOW)
            dupper = (dmid * act).astype(LOW)
            for at, rel in enumerate(rels):
                rows, some_rows = pl.ds(row(rel), local), slice(at * local, (at + 1) * local)
                hidden[rows, pl.ds(first, wide)] = value[some_rows]
                dgu[rows, pl.ds(first, wide)] = dgate[some_rows]
                dgu[rows, pl.ds(ff + first, wide)] = dupper[some_rows]
            return 0

        lax.fori_loop(0, ff // wide, some, 0)

    middle(0)
    for step in range(1, half + 1):
        ring.advance(step)
        middle(step)

    def back_part(rels, begin, end):
        def some(at, _):
            value = dot_nt(block_rows(dgu, rels, local, ranks), weights[at, :, : 2 * ff])
            term[: len(rels) * local, pl.ds(pl.multiple_of(at * deep, deep), deep)] = value
            return 0

        lax.fori_loop(begin, end, some, 0)

    def out_part(rels, begin, end):
        def some(at, _):
            value = dot_nt(block_rows(hidden, rels, local, ranks), weights[at, :, 2 * ff :])
            term[: len(rels) * local, pl.ds(pl.multiple_of(at * deep, deep), deep)] = value
            return 0

        lax.fori_loop(begin, end, some, 0)

    def weight_grads(first, count):
        def some(at, _):
            cols = pl.ds(pl.multiple_of(at * deep, deep), deep)
            grads[at, :, : 2 * ff] = dot_tn(held[:, cols], dgu[...]).astype(LOW)
            grads[at, :, 2 * ff :] = dot_tn(dy_all[:, cols], hidden[...]).astype(LOW)
            return 0

        lax.fori_loop(first, first + count, some, 0)

    back = RingSum(back_part, term, out_buf, in_buf, local, ranks, sems[2], sems[3], right, left)
    out = RingSum(out_part, term, y_out, y_in, local, ranks, sems[4], sems[5], right, left)
    for step in range(1, half + 1):
        back.compute(step)
        back.launch(step)
        out.compute(step)
        out.launch(step)
        made, passed, summed = (((), (0, 1), (2, 3), ()), ((), (), (0, 1), (2, 3)), ((), (), (), (0, 1)))
        for piece in (pieces[at] for at in made[step - 1]):
            weight_grads(piece.begin, piece.count)
            piece.first()
        for at in passed[step - 1]:
            pieces[at].second()
        for at in summed[step - 1]:
            pieces[at].third()
    back.compute(half + 1)
    loads[2].wait()
    back.arrive_last()

    def finish_back(at, _):
        begin = pl.multiple_of(at * 32, 32)
        rows = pl.ds(begin, 32)
        value = resid[rows]
        inv = rows_scaled(value)[1]
        grad = back.last(begin, 32)
        full = out_grad[rows].astype(jnp.float32) + rows_scaled_back(value, inv, grad)
        dresid[rows] = full
        dresid_low[rows] = full.astype(LOW)
        return 0

    lax.fori_loop(0, local // 32, finish_back, 0)
    out.compute(half + 1)
    out.arrive_last()

    def finish_out(at, _):
        begin = pl.multiple_of(at * 32, 32)
        rows = pl.ds(begin, 32)
        block_out[rows] = (resid[rows] + out.last(begin, 32)).astype(LOW)
        return 0

    lax.fori_loop(0, local // 32, finish_out, 0)
    ring.finish()
    for piece in pieces[2:]:
        piece.third()
    back.finish()
    out.finish()
    for piece in pieces:
        piece.finish()


def back_kernel(
    ranks, kv_heads, tokens, dresid_low, query_gain, key_gain, own_out, first_in_in, block_in,
    qkv_in, cos_in, sin_in, q_in, k_in, v_in, prob_in, dresid_in, mlp_own, out_all,
    tokens_grad, gains, out_grad, mlp_sums, attn_sums,
    grads, from_core, from_y, own_grads, query_gain_grad, key_gain_grad,
    tile, tiles_in, tile_sum, tile_sums_in, dob, dout, dk, dv, dqkv,
    first_in, attn_block, qkv, cosv, sinv, q_low, k_low, v_low, prob, dresid, term, out_buf, in_buf,
    o_grads, o_core, o_y, o_own, o_term, o_out, o_in, *sems,
):
    local, width = tokens.shape
    rows = local * ranks
    half = ranks // 2
    size = cosv.shape[1]
    heads = q_low.shape[0]
    share = heads // kv_heads
    scale = 1.0 / math.sqrt(size)
    cols = (heads + 2 * kv_heads) * size
    deep = attn_block.shape[1]
    o_cols = heads * size
    right, left = neighbours(ranks)
    seq, dp = lax.axis_index("seq"), lax.axis_index("dp")
    own = mlp_own.shape[1]
    copies = lax.axis_size("dp")
    row = functools.partial(block_row, local=local, ranks=ranks)
    place = ring_place(seq, ranks)
    out_piece = Reduce(o_grads, o_core, o_y, o_own, own, 0, ranks, pl.ds(0, width), sems[4:6])
    qkv_piece = Reduce(grads, from_core, from_y, own_grads, own, 0, ranks, pl.ds(0, cols), sems[6:8])
    third = mlp_own.shape[2] // 3
    mlp_ways = [
        Deliver(mlp_own, mlp_sums, pl.ds(at * third, third), ranks, [*sems[8:11], *sems[22:28]][3 * at : 3 * at + 3])
        for at in range(3)
    ]
    dob_send, dob_recv = sems[0:2]
    qkv_way = Deliver(own_grads, attn_sums, pl.ds(0, cols), ranks, sems[14:17])
    peers = [(lax.rem(seq + step, ranks), dp) for step in range(1, ranks)]
    peers += [(seq, lax.rem(dp + step, copies)) for step in range(1, copies)]
    knock(peers)
    local_sems = sems[21]
    loads = {}
    for at, (name, src, dst) in enumerate(
        (
            ("out", out_all, o_grads), ("block", block_in, attn_block), ("v", v_in, v_low),
            ("prob", prob_in, prob), ("k", k_in, k_low), ("q", q_in, q_low), ("cos", cos_in, cosv),
            ("sin", sin_in, sinv), ("qkv", qkv_in, qkv), ("first", first_in_in, first_in),
            ("dresid", dresid_in, dresid),
        )
    ):
        loads[name] = move(src, dst, local_sems.at[at])
    answered(peers)
    loads["out"].wait()

    def columns_of(rank):
        return pl.ds(pl.multiple_of(rank * o_cols, o_cols), o_cols)

    def owner(rel):
        return ring_seq(lax.rem(place + rel, ranks), ranks)

    def exchange(rel):
        to = owner(rel)
        return push(
            dob.at[:, columns_of(to)], dout.at[pl.ds(row(0), local)], dob_send.at[rel], dob_recv.at[rel], (to, dp)
        )

    def project(rel):
        some = columns_of(owner(rel))
        dob[:, some] = dot_nn(dresid_low[...], o_grads[:, :, some].reshape(width, o_cols)).astype(LOW)

    for rel in (*ring_order(ranks)[1:][::-1], 0):
        project(rel)
        if rel:
            exchange(rel).start()
    dout[pl.ds(row(0), local)] = dob[:, columns_of(seq)]

    def out_grads(at, _):
        some_cols = pl.ds(pl.multiple_of(at * deep, deep), deep)
        o_grads[at] = dot_tn(dresid_low[:, some_cols], own_out[...]).astype(LOW)
        return 0

    lax.fori_loop(0, ranks, out_grads, 0)
    mlp_ways[0].start()
    out_piece.first()
    out_piece.second()
    for rel in range(1, ranks):
        exchange(rel).wait_recv()
    for name in ("v", "prob", "k", "q", "cos", "sin", "qkv"):
        loads[name].wait()
    mlp_ways[1].start()
    tall = rows // half
    query_gain_grad[...] = jnp.zeros_like(query_gain_grad)
    key_gain_grad[...] = jnp.zeros_like(key_gain_grad)

    def unrotated(grad, column, rows_at, gain, gain_grad_ref):
        grad = grad * cosv[rows_at] - turn(grad) * sinv[rows_at]
        value = qkv[rows_at, column * size : (column + 1) * size]
        normal, inv = rows_scaled(value)
        gain_grad_ref[...] += jnp.sum(grad * normal, 0, keepdims=True)
        back = rows_scaled_back(value, inv, grad * gain[...])
        dqkv[rows_at, column * size : (column + 1) * size] = back.astype(LOW)

    for head in range(heads):
        group = head // share

        def one(piece, _):
            rows_at = pl.ds(pl.multiple_of(piece * tall, tall), tall)
            weight = prob[head, rows_at]
            grad = dout[rows_at, head * size : (head + 1) * size]
            dprob = dot_nt(grad, v_low[group])
            full = weight.astype(jnp.float32)
            delta = jnp.sum(full * dprob, -1, keepdims=True)
            dscore = (full * (dprob - delta)).astype(LOW)
            dq = dot_nn(dscore, k_low[group]) * scale
            dk_add = dot_tn(dscore, q_low[head, rows_at]) * scale
            dv_add = dot_tn(weight, grad)
            dk[group] += dk_add
            dv[group] += dv_add
            unrotated(dq, head, rows_at, query_gain, query_gain_grad)
            return 0

        if head % share == 0:
            dk[group] = jnp.zeros_like(dk[group])
            dv[group] = jnp.zeros_like(dv[group])
        lax.fori_loop(0, half, one, 0)
        if head == 0:
            mlp_ways[2].start()
    for group in range(kv_heads):
        def one_key(piece, _):
            rows_at = pl.ds(pl.multiple_of(piece * tall, tall), tall)
            unrotated(dk[group, rows_at], heads + group, rows_at, key_gain, key_gain_grad)
            at = (heads + kv_heads + group) * size
            dqkv[rows_at, at : at + size] = dv[group, rows_at].astype(LOW)
            return 0

        lax.fori_loop(0, half, one_key, 0)

    def part(rels, begin, end):
        def some(at, _):
            value = dot_nt(block_rows(dqkv, rels, local, ranks), attn_block[at])
            term[: len(rels) * local, pl.ds(pl.multiple_of(at * deep, deep), deep)] = value
            return 0

        lax.fori_loop(begin, end, some, 0)

    def qkv_grads(at, _):
        some_cols = pl.ds(pl.multiple_of(at * deep, deep), deep)
        grads[at] = dot_tn(first_in[:, some_cols], dqkv[...]).astype(LOW)
        return 0

    def to_ranks(step):
        peer = lax.rem(seq + step, ranks)
        return push(tile, tiles_in.at[seq], sems[17].at[step], sems[18].at[step], (peer, dp))

    def to_copies(step):
        peer = lax.rem(dp + step, copies)
        return push(
            tile_sum, tile_sums_in.at[dp], sems[19].at[step], sems[20].at[step], (seq, peer)
        )

    tile[0:1] = query_gain_grad[...]
    tile[1:2] = key_gain_grad[...]
    tile[2:] = jnp.zeros((tile.shape[0] - 2, size), jnp.float32)
    for step in range(1, ranks):
        to_ranks(step).start()
    tiles_in[seq] = tile[...]
    loads["block"].wait()

    def out_part(rels, begin, end):
        for at, rel in enumerate(rels):
            o_term[at * own : (at + 1) * own] = o_own[owner(rel)].astype(jnp.float32)

    out_total = RingSum(out_part, o_term, o_out, o_in, own, ranks, sems[30], sems[31], right, left)
    totals = two_sums(part, term, out_buf, in_buf, local, ranks, [*sems[2:4], *sems[28:30]], right, left)
    for step in range(1, half + 1):
        for total in totals:
            total.compute(step)
            total.launch(step)
        if step == 1:
            loads["first"].wait()
            lax.fori_loop(0, ranks, qkv_grads, 0)
            qkv_piece.first()
            qkv_piece.second()
        if step == 2:
            out_piece.third()
            for other in range(1, ranks):
                to_ranks(other).wait_recv()
            tile_sum[...] = jnp.sum(tiles_in[...], 0)
            for other in range(1, copies):
                to_copies(other).start()
            tile_sums_in[dp] = tile_sum[...]
        if step == half - 1:
            for other in range(1, copies):
                to_copies(other).wait_recv()
            gains[...] = jnp.sum(tile_sums_in[...], 0)
        if step > 1:
            out_total.compute(step - 1)
            out_total.launch(step - 1)
    out_total.compute(half)
    out_total.launch(half)
    qkv_piece.third()
    qkv_way.start()
    for total in totals:
        total.compute(half + 1)
    loads["dresid"].wait()
    for total in totals:
        total.arrive_last()

    def last(at, _):
        begin = pl.multiple_of(at * 32, 32)
        rows_at = pl.ds(begin, 32)
        value = tokens[rows_at].astype(jnp.float32)
        inv = rows_scaled(value)[1]
        grad = jnp.concatenate([total.last(begin, 32) for total in totals], 1)
        tokens_grad[rows_at] = dresid[rows_at] + rows_scaled_back(value, inv, grad)
        return 0

    lax.fori_loop(0, local // 32, last, 0)
    out_total.compute(half + 1)
    out_total.arrive_last()
    out_grad[...] = out_total.last(0, own)
    for step in range(1, ranks):
        to_ranks(step).wait_send()
    for step in range(1, copies):
        to_copies(step).wait_send()
    out_total.finish()
    for rel in range(1, ranks):
        exchange(rel).wait_send()
    for total in totals:
        total.finish()
    out_piece.finish()
    qkv_piece.finish()
    for way in mlp_ways:
        way.finish()
    qkv_way.finish()


def leave_kernel(
    attn_sums, mlp_sums, gains, attn_gain, mlp_gain, w_query, w_key, w_value, w_gate, w_up,
    query_out, key_out, value_out, gate_out, up_out, down_out, attn_out, mlp_out,
    head_query_out, head_key_out,
):
    own = attn_gain.shape[1]
    same = lax.broadcasted_iota(jnp.int32, (own, own), 0) == lax.broadcasted_iota(jnp.int32, (own, own), 1)

    @pl.when(pl.program_id(0) == 0)
    def _():
        attn_out[...] = jnp.zeros_like(attn_out)
        mlp_out[...] = jnp.zeros_like(mlp_out)
        head_query_out[...] = gains[0:1]
        head_key_out[...] = gains[1:2]

    for sums, gain, gain_out, parts in (
        (attn_sums, attn_gain, attn_out, ((query_out, w_query), (key_out, w_key), (value_out, w_value))),
        (mlp_sums, mlp_gain, mlp_out, ((gate_out, w_gate), (up_out, w_up), (down_out, None))),
    ):
        scale = jnp.sum(jnp.where(same, gain[...], 0.0), 1, keepdims=True)
        for rank in range(sums.shape[0]):
            at = 0
            for out, weight in parts:
                each = out.shape[1] // sums.shape[0]
                cols = slice(rank * each, (rank + 1) * each)
                value = sums[rank, :, at : at + each].astype(jnp.float32)
                at += each
                if weight is None:
                    out[:, cols] = value
                    continue
                out[:, cols] = value * scale
                inner = jnp.sum(value * weight[:, cols].astype(jnp.float32), 1, keepdims=True)
                gain_out[...] += jnp.sum(jnp.where(same, inner, 0.0), 0, keepdims=True)


VM = pl.BlockSpec(memory_space=pltpu.VMEM)
SM = pl.BlockSpec(memory_space=pltpu.SMEM)
ANY = pl.BlockSpec(memory_space=pl.ANY)


def call(kernel, number, ins, outs, scratch, operands):
    return pl.pallas_call(
        kernel,
        out_shape=[jax.ShapeDtypeStruct(shape, dtype) for shape, dtype, _ in outs],
        in_specs=ins,
        out_specs=[spec for _, _, spec in outs],
        scratch_shapes=scratch,
        compiler_params=pltpu.CompilerParams(
            collective_id=number, has_side_effects=True, vmem_limit_bytes=LIMIT
        ),
    )(*operands)


def columns_body(
    tokens,
    out_grad,
    span_order,
    doc_starts,
    w_query,
    w_key,
    w_value,
    w_output,
    attn_gain,
    query_gain,
    key_gain,
    w_gate,
    w_up,
    w_down,
    mlp_gain,
):
    ranks = lax.axis_size("seq")
    copies = lax.axis_size("dp")
    _, local, width = tokens.shape
    rows = local * ranks
    size = query_gain.shape[0]
    kv_heads = w_key.shape[1] // size // ranks
    heads = w_query.shape[1] // size // ranks
    q_cols, kv_cols = heads * size, kv_heads * size
    qkv_cols = q_cols + 2 * kv_cols
    ff = w_gate.shape[1] // ranks
    own = width // (ranks * copies)
    deep = own * copies
    half = ranks // 2
    f32, i32 = jnp.float32, jnp.int32
    exponents = np.arange(size) % (size // 2) * (-2.0 / size * math.log(1000000.0))
    freqs = jnp.asarray(np.exp(exponents)[None], f32)
    q_gain, k_gain = query_gain[None], key_gain[None]
    (
        resid, second, cosv, sinv, q_low, k_low, v_low, own_out, first_in, qkv, attn_block, dy_all, prob, mlp_block,
        out_all,
    ) = call(
        functools.partial(first_kernel, ranks, kv_heads),
        1,
        [SM, SM] + [VM] * 11 + [ANY] * 3,
        [
            ((local, width), f32, VM),
            ((local, width), LOW, VM),
            ((rows, size), f32, VM),
            ((rows, size), f32, VM),
            ((heads, rows, size), LOW, VM),
            ((kv_heads, rows, size), LOW, VM),
            ((kv_heads, rows, size), LOW, VM),
            ((local, q_cols * ranks), LOW, VM),
            ((rows, width), LOW, ANY),
            ((rows, qkv_cols), f32, ANY),
            ((ranks, deep, qkv_cols), LOW, ANY),
            ((rows, width), LOW, ANY),
            ((heads, rows, rows), LOW, ANY),
            ((ranks, deep, 3 * ff), LOW, ANY),
            ((ranks, deep, q_cols * ranks), LOW, ANY),
        ],
        [
            pltpu.VMEM((rows, width), LOW),
            pltpu.VMEM((rows, width), LOW),
            pltpu.VMEM((rows, qkv_cols), f32),
            pltpu.VMEM((ranks, deep, qkv_cols), LOW),
            pltpu.VMEM((ranks, own, qkv_cols), LOW),
            pltpu.VMEM((ranks, own, 3 * ff), LOW),
        ]
        + [pltpu.VMEM((own, ff * ranks), LOW)] * 3
        + [
            pltpu.VMEM((rows, width), LOW),
            pltpu.VMEM((heads, rows, rows), LOW),
            pltpu.VMEM((rows, 1), i32),
            pltpu.VMEM((rows, 1), i32),
            pltpu.VMEM((1, rows), i32),
            pltpu.VMEM((rows, q_cols), LOW),
            pltpu.VMEM((ranks, deep, q_cols * ranks), LOW),
        ]
        + ring_sems(ranks)
        + [pltpu.SemaphoreType.DMA((ranks,))] * 2
        + line_sems(ranks)
        + whole_sems(ranks)[:4]
        + spread_sems(ranks) * 4
        + [pltpu.SemaphoreType.DMA((heads * half + 8,))]
        + whole_sems(ranks)[4:],
        (
            span_order, doc_starts, tokens[0], out_grad[0], freqs, attn_gain[None], mlp_gain[None], q_gain, k_gain,
            w_query, w_key, w_value, w_output, w_gate, w_up, w_down,
        ),
    )
    block_out, dresid, dresid_low, mlp_own = call(
        functools.partial(mlp_kernel, ranks),
        2,
        [VM, VM, ANY, ANY, ANY],
        [
            ((local, width), LOW, VM),
            ((local, width), f32, VM),
            ((local, width), LOW, VM),
            ((ranks, own, 3 * ff), LOW, VM),
        ],
        [pltpu.VMEM((ranks, deep, 3 * ff), LOW)]
        + reduce_bufs(ranks, own, 3 * ff)
        + [
            pltpu.VMEM((rows, width), LOW),
            pltpu.VMEM((ranks, deep, 3 * ff), LOW),
            pltpu.VMEM((rows, ff), LOW),
            pltpu.VMEM((rows, 2 * ff), LOW),
            pltpu.VMEM((local, width), f32),
            pltpu.VMEM((rows, width), LOW),
        ]
        + sum_bufs(local, ranks, width)
        + sum_bufs(local, ranks, width)[1:]
        + [pltpu.SemaphoreType.DMA((3,))]
        + ring_sems(ranks) * 3
        + reduce_sems() * 4,
        (second, out_grad[0], resid, dy_all, mlp_block),
    )
    tokens_grad, gains, wo_grad, mlp_sums, attn_sums = call(
        functools.partial(back_kernel, ranks, kv_heads),
        3,
        [VM] * 5 + [ANY] * 12,
        [
            ((local, width), f32, VM),
            ((8, size), f32, VM),
            ((own, q_cols * ranks), f32, VM),
            ((ranks, own, 3 * ff), LOW, ANY),
            ((ranks, own, qkv_cols), LOW, VM),
        ],
        [pltpu.VMEM((ranks, deep, qkv_cols), LOW)]
        + reduce_bufs(ranks, own, qkv_cols)
        + [
            pltpu.VMEM((ranks, own, qkv_cols), LOW),
            pltpu.VMEM((1, size), f32),
            pltpu.VMEM((1, size), f32),
            pltpu.VMEM((8, size), f32),
            pltpu.VMEM((ranks, 8, size), f32),
            pltpu.VMEM((8, size), f32),
            pltpu.VMEM((copies, 8, size), f32),
            pltpu.VMEM((local, q_cols * ranks), LOW),
            pltpu.VMEM((rows, q_cols), LOW),
            pltpu.VMEM((kv_heads, rows, size), f32),
            pltpu.VMEM((kv_heads, rows, size), f32),
            pltpu.VMEM((rows, qkv_cols), LOW),
            pltpu.VMEM((rows, width), LOW),
            pltpu.VMEM((ranks, deep, qkv_cols), LOW),
            pltpu.VMEM((rows, qkv_cols), f32),
            pltpu.VMEM((rows, size), f32),
            pltpu.VMEM((rows, size), f32),
            pltpu.VMEM((heads, rows, size), LOW),
            pltpu.VMEM((kv_heads, rows, size), LOW),
            pltpu.VMEM((kv_heads, rows, size), LOW),
            pltpu.VMEM((heads, rows, rows), LOW),
            pltpu.VMEM((local, width), f32),
        ]
        + sum_bufs(local, ranks, width)
        + [pltpu.VMEM((ranks, deep, q_cols * ranks), LOW)]
        + reduce_bufs(ranks, own, q_cols * ranks)
        + [pltpu.VMEM((ranks, own, q_cols * ranks), LOW)]
        + sum_bufs(own, ranks, q_cols * ranks)
        + [pltpu.SemaphoreType.DMA((ranks,))] * 2
        + ring_sems(ranks)
        + reduce_sems() * 2
        + deliver_sems(ranks) * 3
        + [pltpu.SemaphoreType.DMA((ranks,))] * 2
        + [pltpu.SemaphoreType.DMA((copies,))] * 2
        + [pltpu.SemaphoreType.DMA((11,))]
        + deliver_sems(ranks) * 2
        + ring_sems(ranks) * 2,
        (
            tokens[0], dresid_low, q_gain, k_gain, own_out, first_in, attn_block, qkv, cosv, sinv, q_low, k_low,
            v_low, prob, dresid, mlp_own, out_all,
        ),
    )
    whole = pl.BlockSpec((1, own), lambda at: (0, 0))
    each = (q_cols, kv_cols, kv_cols, ff, ff, ff)
    many = 2
    columns = [pl.BlockSpec((own, many * cols), lambda at: (0, at)) for cols in each]
    head = pl.BlockSpec((1, size), lambda at: (0, 0))
    *grads, dga, dgm, dgq, dgk = pl.pallas_call(
        leave_kernel,
        grid=(ranks // many,),
        out_shape=[jax.ShapeDtypeStruct((own, cols * ranks), f32) for cols in each]
        + [jax.ShapeDtypeStruct((1, own), f32)] * 2
        + [jax.ShapeDtypeStruct((1, size), f32)] * 2,
        in_specs=[
            pl.BlockSpec((many, own, qkv_cols), lambda at: (at, 0, 0)),
            pl.BlockSpec((many, own, 3 * ff), lambda at: (at, 0, 0)),
            pl.BlockSpec((8, size), lambda at: (0, 0)),
            whole,
            whole,
            *columns[:3],
            *columns[3:5],
        ],
        out_specs=columns + [whole, whole, head, head],
    )(attn_sums, mlp_sums, gains, attn_gain[None], mlp_gain[None], w_query, w_key, w_value, w_gate, w_up)
    return (
        block_out[None], tokens_grad[None], *grads[:3], wo_grad, dga[0], dgq[0], dgk[0], *grads[3:], dgm[0],
    )


def body(*args):
    tokens, w_key, query_gain = args[0], args[5], args[9]
    groups = w_key.shape[1] // query_gain.shape[0]
    ranks = lax.axis_size("seq")
    if tokens.shape[0] == 1 and ranks % 2 == 0 and groups % ranks == 0 and lax.axis_size("dp") == 4:
        return columns_body(*args)
    return gathered_body(*args)


def solution(mesh):
    return jax.shard_map(
        body,
        mesh=mesh,
        in_specs=(
            P("dp", "seq", None),
            P("dp", "seq", None),
            P(),
            P("dp", None),
            P(("seq", "dp"), None),
            P(("seq", "dp"), None),
            P(("seq", "dp"), None),
            P(("seq", "dp"), None),
            P(("seq", "dp")),
            P(),
            P(),
            P(("seq", "dp"), None),
            P(("seq", "dp"), None),
            P(("seq", "dp"), None),
            P(("seq", "dp")),
        ),
        out_specs=(
            P("dp", "seq", None),
            P("dp", "seq", None),
            P(("seq", "dp"), None),
            P(("seq", "dp"), None),
            P(("seq", "dp"), None),
            P(("seq", "dp"), None),
            P(("seq", "dp")),
            P(),
            P(),
            P(("seq", "dp"), None),
            P(("seq", "dp"), None),
            P(("seq", "dp"), None),
            P(("seq", "dp")),
        ),
        check_vma=False,
    )
```

profile of v0, /device:TPU:24, one launch (start us, length us, event | category | flops | bytes accessed | tf_op | source)
XLA Modules:
  0.0 481.4 jit_solution(12464096234874609444)
XLA Ops:
  0.6 180.3 %shard_map.255 = (f32[128,2048]{1,0:T(8,128)}, bf16[128,2048]{1,0:T(8,128)(2,1)}, f32[1024,128]{1,0:T(8,128)}, f32[1024,128]{1,0:T(8,128)}, bf16[2,1024,128]{2,1...) custom-call(s32[16]{0:T(128)} %order.1, ...), custom_call_target="tpu_custom_call" | custom-call | tf_op jit(solution)/shard_map/pallas_call | solution.py:1503
  181.0 147.6 %shard_map.256 = (bf16[128,2048]{1,0:T(8,128)(2,1)}, f32[128,2048]{1,0:T(8,128)}, bf16[128,2048]{1,0:T(8,128)(2,1)}, bf16[8,64,2304]{2,1,0:T(8,128)(2,1)}) custom-call(bf16[128,2048]{1,0:T(8,128)(2,1)} %get-tuple-element.47.second, bf16[128,2048]{1,0:T(8,128)(2,1)} %bitcast.13, f32[128,2048]{1,0:T(8,128)} %get-tuple-element.48.rest, ...), custom_call_target="tpu_custom_call" | custom-call | tf_op jit(solution)/shard_map/pallas_call | solution.py:1503
  328.6 144.5 %shard_map.257 = (f32[128,2048]{1,0:T(8,128)}, f32[8,128]{1,0:T(8,128)}, f32[64,2048]{1,0:T(8,128)}, bf16[8,64,2304]{2,1,0:T(8,128)(2,1)}, bf16[8,64,512]{2,1,0:T(8,128)(2,1)}) custom-call(bf16[128,2048]{1,0:T(8,128)(2,1)} %bitcast.15, bf16[128,2048]{1,0:T(8,128)(2,1)} %get-tuple-element.52.dresid_low, f32[1,128]{1,0:T(1,128)} %bitcast.19, ...), custom_call_target="tpu_custom_call" | custom-call | tf_op jit(solution)/shard_map/pallas_call | solution.py:1503
  473.1 0.0 copy-start.1
  473.1 0.0 copy-start
  473.2 5.6 %shard_map.258 = (f32[64,2048]{1,0:T(8,128)}, f32[64,1024]{1,0:T(8,128)}, f32[64,1024]{1,0:T(8,128)}, f32[64,6144]{1,0:T(8,128)}, f32[64,6144]{1,0:T(8,128)}, /*...) custom-call(bf16[8,64,512]{2,1,0:T(8,128)(2,1)} %get-tuple-element.67.attn_sum, ...), custom_call_target="tpu_custom_call" | custom-call | tf_op jit(solution)/shard_map/pallas_call | solution.py:1691
  478.8 0.0 copy-start.2
  478.8 0.0 copy-done.1
  478.8 0.8 copy.32
  479.6 0.0 copy-done
  479.6 1.0 copy.33
  480.6 0.0 copy-done.2
  480.6 0.8 copy.34
Async XLA Ops:
  473.1 5.7 %copy-start.1 = (bf16[128,2048]{1,0:T(8,128)(2,1)S(1)}, bf16[128,2048]{1,0:T(8,128)(2,1)}, u32[]{:S(2)}) copy-start(bf16[128,2048]{1,0:T(8,128)(2,1)} %get-tuple-element.51) | copy-start | bytes 1572868
  473.1 6.4 %copy-start = (f32[128,2048]{1,0:T(8,128)S(1)}, f32[128,2048]{1,0:T(8,128)}, u32[]{:S(2)}) copy-start(f32[128,2048]{1,0:T(8,128)} %get-tuple-element.66) | copy-start | bytes 3145732
  478.8 1.8 copy-start.2
where the time goes:
time: 482 us; the launch traced here: 481 us
  Pallas kernels  478 us (99%)
    pallas_call x3, Pallas kernels, call(): pl.pallas_call(kernel, out_shape=[jax.ShapeDtypeStruct(shape, dtype) for...  472 us

commit v1 on v0

--- a/solution.py
+++ b/solution.py
@@ -1182,7 +1182,7 @@
         back.launch(step)
         out.compute(step)
         out.launch(step)
-        made, passed, summed = (((), (0, 1), (2, 3), ()), ((), (), (0, 1), (2, 3)), ((), (), (), (0, 1)))
+        made, passed, summed = (((0, 1), (2, 3), (), ()), ((), (0, 1), (2, 3), ()), ((), (), (0, 1), (2, 3)))
         for piece in (pieces[at] for at in made[step - 1]):
             weight_grads(piece.begin, piece.count)
             piece.first()
@@ -1217,8 +1217,6 @@
 
     lax.fori_loop(0, local // 32, finish_out, 0)
     ring.finish()
-    for piece in pieces[2:]:
-        piece.third()
     back.finish()
     out.finish()
     for piece in pieces:

time: 482 us -> 471 us (0.977)
  Pallas kernels: 478 us -> 468 us
    pallas_call x3, Pallas kernels: 472 us -> 462 us  [call(): pl.pallas_call(kernel, out_shape=[jax.ShapeDtypeStruct(shape, dtype) for...]
where the time goes in v1:
time: 471 us
  Pallas kernels  468 us (99%)
    pallas_call x3, Pallas kernels, call(): pl.pallas_call(kernel, out_shape=[jax.ShapeDtypeStruct(shape, dtype) for...  462 us

profile of v1, /device:TPU:24, one launch (start us, length us, event | category | flops | bytes accessed | tf_op | source)
XLA Modules:
  0.0 471.0 jit_solution(12455320034319804101)
XLA Ops:
  0.6 180.3 %shard_map.255 = (f32[128,2048]{1,0:T(8,128)}, bf16[128,2048]{1,0:T(8,128)(2,1)}, f32[1024,128]{1,0:T(8,128)}, f32[1024,128]{1,0:T(8,128)}, bf16[2,1024,128]{2,1...) custom-call(s32[16]{0:T(128)} %order.1, ...), custom_call_target="tpu_custom_call" | custom-call | tf_op jit(solution)/shard_map/pallas_call | solution.py:1501
  181.0 135.5 %shard_map.256 = (bf16[128,2048]{1,0:T(8,128)(2,1)}, f32[128,2048]{1,0:T(8,128)}, bf16[128,2048]{1,0:T(8,128)(2,1)}, bf16[8,64,2304]{2,1,0:T(8,128)(2,1)}) custom-call(bf16[128,2048]{1,0:T(8,128)(2,1)} %get-tuple-element.47.second, bf16[128,2048]{1,0:T(8,128)(2,1)} %bitcast.13, f32[128,2048]{1,0:T(8,128)} %get-tuple-element.48.rest, ...), custom_call_target="tpu_custom_call" | custom-call | tf_op jit(solution)/shard_map/pallas_call | solution.py:1501
  316.5 146.2 %shard_map.257 = (f32[128,2048]{1,0:T(8,128)}, f32[8,128]{1,0:T(8,128)}, f32[64,2048]{1,0:T(8,128)}, bf16[8,64,2304]{2,1,0:T(8,128)(2,1)}, bf16[8,64,512]{2,1,0:T(8,128)(2,1)}) custom-call(bf16[128,2048]{1,0:T(8,128)(2,1)} %bitcast.15, bf16[128,2048]{1,0:T(8,128)(2,1)} %get-tuple-element.52.dresid_low, f32[1,128]{1,0:T(1,128)} %bitcast.19, ...), custom_call_target="tpu_custom_call" | custom-call | tf_op jit(solution)/shard_map/pallas_call | solution.py:1501
  462.7 0.0 copy-start.1
  462.7 0.0 copy-start
  462.8 5.6 %shard_map.258 = (f32[64,2048]{1,0:T(8,128)}, f32[64,1024]{1,0:T(8,128)}, f32[64,1024]{1,0:T(8,128)}, f32[64,6144]{1,0:T(8,128)}, f32[64,6144]{1,0:T(8,128)}, /*...) custom-call(bf16[8,64,512]{2,1,0:T(8,128)(2,1)} %get-tuple-element.67.attn_sum, ...), custom_call_target="tpu_custom_call" | custom-call | tf_op jit(solution)/shard_map/pallas_call | solution.py:1689
  468.4 0.0 copy-start.2
  468.4 0.0 copy-done.1
  468.4 0.8 copy.32
  469.2 0.0 copy-done
  469.2 1.0 copy.33
  470.2 0.0 copy-done.2
  470.2 0.8 copy.34
Async XLA Ops:
  462.7 5.7 %copy-start.1 = (bf16[128,2048]{1,0:T(8,128)(2,1)S(1)}, bf16[128,2048]{1,0:T(8,128)(2,1)}, u32[]{:S(2)}) copy-start(bf16[128,2048]{1,0:T(8,128)(2,1)} %get-tuple-element.51) | copy-start | bytes 1572868
  462.7 6.4 %copy-start = (f32[128,2048]{1,0:T(8,128)S(1)}, f32[128,2048]{1,0:T(8,128)}, u32[]{:S(2)}) copy-start(f32[128,2048]{1,0:T(8,128)} %get-tuple-element.66) | copy-start | bytes 3145732
  468.4 1.8 copy-start.2
